TPU v7x, 256 devices: a whole 4x4x8 slice. The times are simulated.
256 devices in a mesh: orb: 4 (over z_lo, core), dom: 64 (over z_hi, y, x).
Axes of the slice: x: 4, y: 4, z: 8 (z_hi: 4, z_lo: 2; z = z_hi * 2 + z_lo), core: 2. Of those that a mesh axis runs over, the one named last changes fastest.
Arguments:
- orbitals: float32 [2, 16, 256, 64, 128], P(None, 'orb', 'dom'), may hold values from -6 to 6
- occupations: int32 [16], P('orb'), may hold values from 1 to 2
- external: float32 [256, 64, 128], P('dom'), may hold values from -2 to 0.5
- control: float32 [2], replicated, may hold values from -2 to 2
Outputs:
- propagated: float32 [2, 16, 256, 64, 128], P(None, 'orb', 'dom')
- hartree: float32 [256, 64, 128], P('dom')
All inputs are finite; a program needn't handle non-finite values.
Results may differ from a plain program's by a relative error of at most 0.00016.
Values sent between devices are 32-bit elements; how exact they have to be, the bound alone decides.
A program may use at most 64 MiB of HBM per device.

v0:
```python
import jax
import jax.numpy as jnp
from jax import lax
from jax.sharding import PartitionSpec as P

STEPS = 2
TERMS = 4
LEVELS = 3
CYCLES = 2
SWEEPS = 2
COARSE = 4


time_step = 0.2
omega = 0.8
coupling = 0.025


def with_halo(block, sides, width):
    for axis, dim in sides:
        count = lax.axis_size(axis)
        forward = [(i, i + 1) for i in range(count - 1)]
        backward = [(target, source) for source, target in forward]
        low = lax.ppermute(
            lax.slice_in_dim(block, block.shape[dim] - width, None, axis=dim), axis, forward
        )
        high = lax.ppermute(lax.slice_in_dim(block, 0, width, axis=dim), axis, backward)
        block = jnp.concatenate([low, block, high], axis=dim)
    return block


def neighbour(field, offset, axis):
    count = field.shape[axis]
    reach = abs(offset)
    widths = [(0, 0)] * field.ndim
    widths[axis] = (reach, reach)
    padded = jnp.pad(field, widths)
    return lax.slice_in_dim(padded, reach + offset, reach + offset + count, axis=axis)


def cross_four(field, first):
    total = jnp.zeros_like(field)
    for axis in (first, first + 1):
        near = neighbour(field, 1, axis) + neighbour(field, -1, axis)
        far = neighbour(field, 2, axis) + neighbour(field, -2, axis)
        total = total + 4.0 / 3.0 * near - 1.0 / 12.0 * far
    return total


def shrink_apply(padded, potential):
    center = padded[:, :, 2:-2]
    near = padded[:, :, 3:-1] + padded[:, :, 1:-3]
    far = padded[:, :, 4:] + padded[:, :, :-4]
    laplace = -7.5 * center + 4.0 / 3.0 * near - 1.0 / 12.0 * far + cross_four(center, 3)
    return -0.5 * laplace + potential * center


def apply_single(term, potential):
    padded = with_halo(term, (("dom", 2),), 2)
    return shrink_apply(padded, potential)


def seven_replicated(field, level):
    padded = with_halo(field, (("dom", 0),), 1)
    beside = padded[2:] + padded[:-2]
    beside = beside + neighbour(field, 1, 1) + neighbour(field, -1, 1)
    beside = beside + neighbour(field, 1, 2) + neighbour(field, -1, 2)
    return (6.0 * field - beside) / 4.0**level


def restrict(field):
    a, b, c = field.shape
    return field.reshape(a // 2, 2, b // 2, 2, c // 2, 2).mean(axis=(1, 3, 5))


def prolong(field):
    return jnp.repeat(jnp.repeat(jnp.repeat(field, 2, 0), 2, 1), 2, 2)


def vcycle(field, source, level, operate):
    relax = omega * 4.0**level / 6.0
    if level == LEVELS - 1:
        for sweep in range(COARSE):
            field = field + relax * (source - operate(field, level))
        return field
    for sweep in range(SWEEPS):
        field = field + relax * (source - operate(field, level))
    coarse = restrict(source - operate(field, level))
    field = field + prolong(vcycle(jnp.zeros_like(coarse), coarse, level + 1, operate))
    for sweep in range(SWEEPS):
        field = field + relax * (source - operate(field, level))
    return field


def per_device(orbitals, occupations, external, control):
    planes = orbitals.shape[2]
    grid_planes = planes * lax.axis_size("dom")
    start = lax.axis_index("dom") * planes
    positions = ((start + jnp.arange(planes, dtype=jnp.int32)).astype(jnp.float32) + 0.5) * (
        2.0 / grid_planes
    ) - 1.0
    dipole = positions[:, None, None]
    weights = occupations.astype(jnp.float32) / (orbitals.shape[1] * lax.axis_size("orb"))
    psi = orbitals
    hartree = jnp.zeros(external.shape, jnp.float32)
    for step in range(STEPS):
        local = jnp.sum(weights[:, None, None, None] * (psi[0] * psi[0] + psi[1] * psi[1]), axis=0)
        source = coupling * lax.psum(local, "orb")
        hartree = jnp.zeros_like(source)
        for cycle in range(CYCLES):
            hartree = vcycle(hartree, source, 0, seven_replicated)
        potential = external + hartree + control[step] * dipole
        term = psi
        total = psi
        for order in range(1, TERMS + 1):
            image = apply_single(term, potential)
            factor = time_step / order
            term = jnp.stack([factor * image[1], -factor * image[0]])
            total = total + term
        psi = total
    return (psi, hartree)


def solution(mesh):
    in_specs = (P(None, "orb", "dom", None, None), P("orb"), P("dom", None, None), P())
    out_specs = (P(None, "orb", "dom", None, None), P("dom", None, None))
    return jax.shard_map(
        per_device, mesh=mesh, in_specs=in_specs, out_specs=out_specs, check_vma=False
    )
```

profile of v0, /device:TPU:94, one launch (start us, length us, event | category | flops | bytes accessed | tf_op | source)
XLA Modules:
  0.0 1085.4 jit_solution(15190468701499575261)
XLA Ops:
  23.7 29.8 %all-reduce.137.cloned.1.call-done = f32[4,64,128]{2,1,0:T(8,128)} async-done(((f32[4,64,128]{2,1,0:T(8,128)}), f32[4,64,128]{2,1,0:T(8,128)}) %all-reduce.137.cloned.1.call-update) | async-done | bytes 131088 | tf_op jit(solution)/shard_map/psum | solution.py:108
  71.3 10.6 collective-permute-start.7
  205.8 10.6 collective-permute-start.25
  234.5 10.6 collective-permute-start.29
  248.9 10.7 collective-permute-start.31
  263.3 10.6 collective-permute-start.33
  277.5 10.6 collective-permute-start.35
  305.7 10.6 collective-permute-start.37
  390.3 13.7 %collective-permute-start.49 = (f32[1,32,64]{2,1,0:T(8,128)S(1)}, f32[1,32,64]{2,1,0:T(8,128)S(1)}, u32[]{:S(2)}, u32[]{:S(2)}) collective-permute-start(f32[1,32,64]{2,1,0:T(8,128)S(1)} %get-tuple-element.113), channel_id=1, source_target_pairs={{0,1},{1,2},{2,3},{3,4},{4,5},{5,6},{6,7},{7,8},{8,9},{9,10},{10,1... | collective-permute-start | bytes 24584 | tf_op jit(solution)/shard_map/ppermute | solution.py:24
  432.8 10.7 collective-permute-start.53
  449.2 10.9 %collective-permute-start.55 = (f32[2,4,2,64,128]{4,3,2,1,0:T(8,128)S(1)}, f32[2,4,2,64,128]{4,3,2,1,0:T(8,128)S(1)}, u32[]{:S(2)}, u32[]{:S(2)}) collective-permute-start(f32[2,4,2,64,128]{4,3,2,1,0:T(8,128)S(1)} %get-tuple-element.53), channel_id=1, source_target_pairs={{0,1},{1,2},{2,3},{3,4},{4,5},{5,6},{6,7},{7,8},{8,9},{9,10},{10,1... | collective-permute-start | bytes 1572872 | tf_op jit(solution)/shard_map/ppermute | solution.py:24
  460.2 24.1 %collective-permute-done.54 = f32[2,4,2,64,128]{4,3,2,1,0:T(8,128)S(1)} collective-permute-done((f32[2,4,2,64,128]{4,3,2,1,0:T(8,128)S(1)}, f32[2,4,2,64,128]{4,3,2,1,0:T(8,128)S(1)}, u32[]{:S(2)}, u32[]{:S(2)}) %collective-permute-start.54) | collective-permute-done | bytes 524320 | tf_op jit(solution)/shard_map/ppermute | solution.py:27
  498.6 15.9 %collective-permute-done.56 = f32[2,4,2,64,128]{4,3,2,1,0:T(8,128)S(1)} collective-permute-done((f32[2,4,2,64,128]{4,3,2,1,0:T(8,128)S(1)}, f32[2,4,2,64,128]{4,3,2,1,0:T(8,128)S(1)}, u32[]{:S(2)}, u32[]{:S(2)}) %collective-permute-start.56) | collective-permute-done | bytes 524320 | tf_op jit(solution)/shard_map/ppermute | solution.py:27
  539.8 42.0 %all-reduce.139.cloned.1.call-done = f32[4,64,128]{2,1,0:T(8,128)} async-done(((f32[4,64,128]{2,1,0:T(8,128)}), f32[4,64,128]{2,1,0:T(8,128)}) %all-reduce.139.cloned.1.call-update) | async-done | bytes 131088 | tf_op jit(solution)/shard_map/psum | solution.py:108
  599.5 10.6 collective-permute-start.65
  628.5 10.6 collective-permute-start.67
  752.6 10.7 collective-permute-start.83
  767.1 10.7 collective-permute-start.85
  781.4 10.6 collective-permute-start.87
  825.1 10.6 collective-permute-start.91
  932.3 10.7 collective-permute-start.105
  992.2 21.8 %collective-permute-done.108 = f32[2,4,2,64,128]{4,3,2,1,0:T(8,128)S(1)} collective-permute-done((f32[2,4,2,64,128]{4,3,2,1,0:T(8,128)S(1)}, f32[2,4,2,64,128]{4,3,2,1,0:T(8,128)S(1)}, u32[]{:S(2)}, u32[]{:S(2)}) %collective-permute-start.108) | collective-permute-done | bytes 524320 | tf_op jit(solution)/shard_map/ppermute | solution.py:27
  1019.5 10.7 collective-permute-start.111
  1030.3 17.8 %collective-permute-done.110 = f32[2,4,2,64,128]{4,3,2,1,0:T(8,128)S(1)} collective-permute-done((f32[2,4,2,64,128]{4,3,2,1,0:T(8,128)S(1)}, f32[2,4,2,64,128]{4,3,2,1,0:T(8,128)S(1)}, u32[]{:S(2)}, u32[]{:S(2)}) %collective-permute-start.110) | collective-permute-done | bytes 524320 | tf_op jit(solution)/shard_map/ppermute | solution.py:27
  (444 shorter events, 722.9 us)
Async XLA Ops:
  7.2 46.3 %all-reduce.137.cloned.1.call-start = ((), (), s32[]{:S(2)}) async-start(), calls=%async_computation | async-start | bytes 262144 | tf_op jit(solution)/shard_map/psum | solution.py:108
  9.9 572.0 %all-reduce.139.cloned.1.call-start = ((), (), s32[]{:S(2)}) async-start(), calls=%async_computation.1 | async-start | bytes 262144 | tf_op jit(solution)/shard_map/psum | solution.py:108
  69.4 24.7 %collective-permute-start.6 = (f32[1,64,128]{2,1,0:T(8,128)S(1)}, f32[1,64,128]{2,1,0:T(8,128)S(1)}, u32[]{:S(2)}, u32[]{:S(2)}) collective-permute-start(f32[1,64,128]{2,1,0:T(8,128)S(1)} %get-tuple-element.92), channel_id=1, source_target_pairs={{1,0},{2,1},{3,2},{4,3},{5,4},{6,5},{7,6},{8,7},{9,8},{10,9},{11,1... | collective-permute-start | bytes 98312 | tf_op jit(solution)/shard_map/ppermute | solution.py:27
  71.3 22.8 %collective-permute-start.7 = (f32[1,64,128]{2,1,0:T(8,128)S(1)}, f32[1,64,128]{2,1,0:T(8,128)S(1)}, u32[]{:S(2)}, u32[]{:S(2)}) collective-permute-start(f32[1,64,128]{2,1,0:T(8,128)S(1)} %get-tuple-element.93), channel_id=1, source_target_pairs={{0,1},{1,2},{2,3},{3,4},{4,5},{5,6},{6,7},{7,8},{8,9},{9,10},{10,1... | collective-permute-start | bytes 98312 | tf_op jit(solution)/shard_map/ppermute | solution.py:24
  81.9 26.2 %collective-permute-start.8 = (f32[1,32,64]{2,1,0:T(8,128)S(1)}, f32[1,32,64]{2,1,0:T(8,128)S(1)}, u32[]{:S(2)}, u32[]{:S(2)}) collective-permute-start(f32[1,32,64]{2,1,0:T(8,128)S(1)} %broadcast.553), channel_id=1, source_target_pairs={{1,0},{2,1},{3,2},{4,3},{5,4},{6,5},{7,6},{8,7},{9,8},{10,9},{11,1... | collective-permute-start | bytes 24584 | tf_op jit(solution)/shard_map/ppermute | solution.py:27
  83.8 24.3 %collective-permute-start.9 = (f32[1,32,64]{2,1,0:T(8,128)S(1)}, f32[1,32,64]{2,1,0:T(8,128)S(1)}, u32[]{:S(2)}, u32[]{:S(2)}) collective-permute-start(f32[1,32,64]{2,1,0:T(8,128)S(1)} %broadcast.553), channel_id=1, source_target_pairs={{0,1},{1,2},{2,3},{3,4},{4,5},{5,6},{6,7},{7,8},{8,9},{9,10},{10,1... | collective-permute-start | bytes 24584 | tf_op jit(solution)/shard_map/ppermute | solution.py:24
  122.0 24.7 %collective-permute-start.12 = (f32[1,32,64]{2,1,0:T(8,128)S(1)}, f32[1,32,64]{2,1,0:T(8,128)S(1)}, u32[]{:S(2)}, u32[]{:S(2)}) collective-permute-start(f32[1,32,64]{2,1,0:T(8,128)S(1)} %get-tuple-element.124), channel_id=1, source_target_pairs={{1,0},{2,1},{3,2},{4,3},{5,4},{6,5},{7,6},{8,7},{9,8},{10,9},{11,1... | collective-permute-start | bytes 24584 | tf_op jit(solution)/shard_map/ppermute | solution.py:27
  123.9 22.8 %collective-permute-start.13 = (f32[1,32,64]{2,1,0:T(8,128)S(1)}, f32[1,32,64]{2,1,0:T(8,128)S(1)}, u32[]{:S(2)}, u32[]{:S(2)}) collective-permute-start(f32[1,32,64]{2,1,0:T(8,128)S(1)} %get-tuple-element.125), channel_id=1, source_target_pairs={{0,1},{1,2},{2,3},{3,4},{4,5},{5,6},{6,7},{7,8},{8,9},{9,10},{10,1... | collective-permute-start | bytes 24584 | tf_op jit(solution)/shard_map/ppermute | solution.py:24
  388.3 22.7 %collective-permute-start.48 = (f32[1,32,64]{2,1,0:T(8,128)S(1)}, f32[1,32,64]{2,1,0:T(8,128)S(1)}, u32[]{:S(2)}, u32[]{:S(2)}) collective-permute-start(f32[1,32,64]{2,1,0:T(8,128)S(1)} %get-tuple-element.112), channel_id=1, source_target_pairs={{1,0},{2,1},{3,2},{4,3},{5,4},{6,5},{7,6},{8,7},{9,8},{10,9},{11,1... | collective-permute-start | bytes 24584 | tf_op jit(solution)/shard_map/ppermute | solution.py:27
  405.0 40.4 %collective-permute-start.1 = (f32[2,4,2,64,128]{4,3,2,1,0:T(8,128)}, f32[2,4,2,64,128]{4,3,2,1,0:T(8,128)S(1)}, u32[]{:S(2)}, u32[]{:S(2)}) collective-permute-start(f32[2,4,2,64,128]{4,3,2,1,0:T(8,128)} %get-tuple-element.57), channel_id=1, source_target_pairs={{0,1},{1,2},{2,3},{3,4},{4,5},{5,6},{6,7},{7,8},{8,9},{9,10},{10,1... | collective-permute-start | bytes 1572872 | tf_op jit(solution)/shard_map/ppermute | solution.py:24
  409.1 36.7 %collective-permute-start = (f32[2,4,2,64,128]{4,3,2,1,0:T(8,128)}, f32[2,4,2,64,128]{4,3,2,1,0:T(8,128)S(1)}, u32[]{:S(2)}, u32[]{:S(2)}) collective-permute-start(f32[2,4,2,64,128]{4,3,2,1,0:T(8,128)} %get-tuple-element.56), channel_id=1, source_target_pairs={{1,0},{2,1},{3,2},{4,3},{5,4},{6,5},{7,6},{8,7},{9,8},{10,9},{11,1... | collective-permute-start | bytes 1572872 | tf_op jit(solution)/shard_map/ppermute | solution.py:27
  447.3 37.1 %collective-permute-start.54 = (f32[2,4,2,64,128]{4,3,2,1,0:T(8,128)S(1)}, f32[2,4,2,64,128]{4,3,2,1,0:T(8,128)S(1)}, u32[]{:S(2)}, u32[]{:S(2)}) collective-permute-start(f32[2,4,2,64,128]{4,3,2,1,0:T(8,128)S(1)} %get-tuple-element.52), channel_id=1, source_target_pairs={{1,0},{2,1},{3,2},{4,3},{5,4},{6,5},{7,6},{8,7},{9,8},{10,9},{11,1... | collective-permute-start | bytes 1572872 | tf_op jit(solution)/shard_map/ppermute | solution.py:27
  449.2 35.1 %collective-permute-start.55 = (f32[2,4,2,64,128]{4,3,2,1,0:T(8,128)S(1)}, f32[2,4,2,64,128]{4,3,2,1,0:T(8,128)S(1)}, u32[]{:S(2)}, u32[]{:S(2)}) collective-permute-start(f32[2,4,2,64,128]{4,3,2,1,0:T(8,128)S(1)} %get-tuple-element.53), channel_id=1, source_target_pairs={{0,1},{1,2},{2,3},{3,4},{4,5},{5,6},{6,7},{7,8},{8,9},{9,10},{10,1... | collective-permute-start | bytes 1572872 | tf_op jit(solution)/shard_map/ppermute | solution.py:24
  486.3 28.2 %collective-permute-start.56 = (f32[2,4,2,64,128]{4,3,2,1,0:T(8,128)S(1)}, f32[2,4,2,64,128]{4,3,2,1,0:T(8,128)S(1)}, u32[]{:S(2)}, u32[]{:S(2)}) collective-permute-start(f32[2,4,2,64,128]{4,3,2,1,0:T(8,128)S(1)} %get-tuple-element.46), channel_id=1, source_target_pairs={{1,0},{2,1},{3,2},{4,3},{5,4},{6,5},{7,6},{8,7},{9,8},{10,9},{11,1... | collective-permute-start | bytes 1572872 | tf_op jit(solution)/shard_map/ppermute | solution.py:27
  488.2 26.2 %collective-permute-start.57 = (f32[2,4,2,64,128]{4,3,2,1,0:T(8,128)S(1)}, f32[2,4,2,64,128]{4,3,2,1,0:T(8,128)S(1)}, u32[]{:S(2)}, u32[]{:S(2)}) collective-permute-start(f32[2,4,2,64,128]{4,3,2,1,0:T(8,128)S(1)} %get-tuple-element.47), channel_id=1, source_target_pairs={{0,1},{1,2},{2,3},{3,4},{4,5},{5,6},{6,7},{7,8},{8,9},{9,10},{10,1... | collective-permute-start | bytes 1572872 | tf_op jit(solution)/shard_map/ppermute | solution.py:24
  930.3 26.1 %collective-permute-start.104 = (f32[1,64,128]{2,1,0:T(8,128)S(1)}, f32[1,64,128]{2,1,0:T(8,128)S(1)}, u32[]{:S(2)}, u32[]{:S(2)}) collective-permute-start(f32[1,64,128]{2,1,0:T(8,128)S(1)} %get-tuple-element.62), channel_id=1, source_target_pairs={{1,0},{2,1},{3,2},{4,3},{5,4},{6,5},{7,6},{8,7},{9,8},{10,9},{11,1... | collective-permute-start | bytes 98312 | tf_op jit(solution)/shard_map/ppermute | solution.py:27
  932.3 24.2 %collective-permute-start.105 = (f32[1,64,128]{2,1,0:T(8,128)S(1)}, f32[1,64,128]{2,1,0:T(8,128)S(1)}, u32[]{:S(2)}, u32[]{:S(2)}) collective-permute-start(f32[1,64,128]{2,1,0:T(8,128)S(1)} %get-tuple-element.63), channel_id=1, source_target_pairs={{0,1},{1,2},{2,3},{3,4},{4,5},{5,6},{6,7},{7,8},{8,9},{9,10},{10,1... | collective-permute-start | bytes 98312 | tf_op jit(solution)/shard_map/ppermute | solution.py:24
  944.2 34.0 %collective-permute-start.60 = (f32[2,4,2,64,128]{4,3,2,1,0:T(8,128)S(1)}, f32[2,4,2,64,128]{4,3,2,1,0:T(8,128)S(1)}, u32[]{:S(2)}, u32[]{:S(2)}) collective-permute-start(f32[2,4,2,64,128]{4,3,2,1,0:T(8,128)S(1)} %get-tuple-element.34), channel_id=1, source_target_pairs={{1,0},{2,1},{3,2},{4,3},{5,4},{6,5},{7,6},{8,7},{9,8},{10,9},{11,1... | collective-permute-start | bytes 1572872 | tf_op jit(solution)/shard_map/ppermute | solution.py:27
  946.2 32.1 %collective-permute-start.61 = (f32[2,4,2,64,128]{4,3,2,1,0:T(8,128)S(1)}, f32[2,4,2,64,128]{4,3,2,1,0:T(8,128)S(1)}, u32[]{:S(2)}, u32[]{:S(2)}) collective-permute-start(f32[2,4,2,64,128]{4,3,2,1,0:T(8,128)S(1)} %get-tuple-element.35), channel_id=1, source_target_pairs={{0,1},{1,2},{2,3},{3,4},{4,5},{5,6},{6,7},{7,8},{8,9},{9,10},{10,1... | collective-permute-start | bytes 1572872 | tf_op jit(solution)/shard_map/ppermute | solution.py:24
  979.9 34.1 %collective-permute-start.108 = (f32[2,4,2,64,128]{4,3,2,1,0:T(8,128)S(1)}, f32[2,4,2,64,128]{4,3,2,1,0:T(8,128)S(1)}, u32[]{:S(2)}, u32[]{:S(2)}) collective-permute-start(f32[2,4,2,64,128]{4,3,2,1,0:T(8,128)S(1)} %get-tuple-element.30), channel_id=1, source_target_pairs={{1,0},{2,1},{3,2},{4,3},{5,4},{6,5},{7,6},{8,7},{9,8},{10,9},{11,1... | collective-permute-start | bytes 1572872 | tf_op jit(solution)/shard_map/ppermute | solution.py:27
  981.8 33.8 %collective-permute-start.109 = (f32[2,4,2,64,128]{4,3,2,1,0:T(8,128)S(1)}, f32[2,4,2,64,128]{4,3,2,1,0:T(8,128)S(1)}, u32[]{:S(2)}, u32[]{:S(2)}) collective-permute-start(f32[2,4,2,64,128]{4,3,2,1,0:T(8,128)S(1)} %get-tuple-element.31), channel_id=1, source_target_pairs={{0,1},{1,2},{2,3},{3,4},{4,5},{5,6},{6,7},{7,8},{8,9},{9,10},{10,1... | collective-permute-start | bytes 1572872 | tf_op jit(solution)/shard_map/ppermute | solution.py:24
  1017.5 30.5 %collective-permute-start.110 = (f32[2,4,2,64,128]{4,3,2,1,0:T(8,128)S(1)}, f32[2,4,2,64,128]{4,3,2,1,0:T(8,128)S(1)}, u32[]{:S(2)}, u32[]{:S(2)}) collective-permute-start(f32[2,4,2,64,128]{4,3,2,1,0:T(8,128)S(1)} %get-tuple-element.24), channel_id=1, source_target_pairs={{1,0},{2,1},{3,2},{4,3},{5,4},{6,5},{7,6},{8,7},{9,8},{10,9},{11,1... | collective-permute-start | bytes 1572872 | tf_op jit(solution)/shard_map/ppermute | solution.py:27
  1019.5 28.6 %collective-permute-start.111 = (f32[2,4,2,64,128]{4,3,2,1,0:T(8,128)S(1)}, f32[2,4,2,64,128]{4,3,2,1,0:T(8,128)S(1)}, u32[]{:S(2)}, u32[]{:S(2)}) collective-permute-start(f32[2,4,2,64,128]{4,3,2,1,0:T(8,128)S(1)} %get-tuple-element.25), channel_id=1, source_target_pairs={{0,1},{1,2},{2,3},{3,4},{4,5},{5,6},{6,7},{7,8},{8,9},{9,10},{10,1... | collective-permute-start | bytes 1572872 | tf_op jit(solution)/shard_map/ppermute | solution.py:24
  1050.0 23.0 %collective-permute-start.112 = (f32[2,4,2,64,128]{4,3,2,1,0:T(8,128)S(1)}, f32[2,4,2,64,128]{4,3,2,1,0:T(8,128)S(1)}, u32[]{:S(2)}, u32[]{:S(2)}) collective-permute-start(f32[2,4,2,64,128]{4,3,2,1,0:T(8,128)S(1)} %get-tuple-element.18), channel_id=1, source_target_pairs={{1,0},{2,1},{3,2},{4,3},{5,4},{6,5},{7,6},{8,7},{9,8},{10,9},{11,1... | collective-permute-start | bytes 1572872 | tf_op jit(solution)/shard_map/ppermute | solution.py:27
  (108 other events, 1633.3 us)
Sparse Core Ops, SparseCore 0:
  11.2 42.2 all-reduce.136
  539.9 41.8 all-reduce.138
where the time goes:
time: 1100 us; the launch traced here: 1090 us
  starting transfers between devices  705 us (64%)
  waiting for transfers between devices  244 us (22%)
  local copies, waits for them, and re-layouts  64.8 us (6%)
  other arithmetic  54.8 us (5%)
  between operations  16.8 us (2%)
    ppermute x57, starting transfers between devices, with_halo(): lax.ppermute(lax.slice_in_dim(block, block.shape[dim] - width, None, axis...  592 us
    ppermute x57, starting transfers between devices, with_halo(): lax.ppermute(lax.slice_in_dim(block, 0, width, axis=dim), axis, backward)  112 us
    ppermute x57, waiting for transfers between devices, with_halo(): lax.ppermute(lax.slice_in_dim(block, 0, width, axis=dim), axis, backward)  112 us
    psum x2, waiting for transfers between devices, per_device(): source = coupling * lax.psum(local, 'orb')  71.8 us
    ppermute x57, waiting for transfers between devices, with_halo(): lax.ppermute(lax.slice_in_dim(block, block.shape[dim] - width, None, axis...  60.5 us
    reshape x4, local copies, waits for them, and re-layouts, restrict(): return field.reshape(a // 2, 2, b // 2, 2, c // 2, 2).mean(axis=(1, 3, 5))  39.9 us
  transfers between devices with their start and end apart: 116, of which 60 were waited for; matrix products, arithmetic and copies ran while one was open for 2% of the time, Pallas kernels for 0%

commit v1 on v0

v1 whole, which is shorter than its diff:
```python
import functools

import jax
import jax.numpy as jnp
from jax import lax
from jax.experimental import pallas as pl
from jax.experimental.pallas import tpu as pltpu
from jax.sharding import PartitionSpec as P

STEPS = 2
TERMS = 4
TIME_STEP = 0.2
COUPLING = 0.025
RELAX = 0.8 / 6.0
KEEP = 0.2

ORB = 4
DOM = 64
RING = 4
GROUPS = DOM // RING
SLAB = 4
GROUP = RING * SLAB
WIDE = 8
NX = DOM * SLAB
NY, NZ = 64, 128
EXT = GROUP + 2 * WIDE
FEXT = SLAB + 2 * WIDE
REACH = 7
SLABS = 2 * REACH + 1
Y1, Y2 = NY // 2, NY // 4
COPIES = 160
HIGH = lax.Precision.HIGHEST


def dot(a, b):
    return jnp.dot(a, b, precision=HIGH, preferred_element_type=jnp.float32)


def iota(shape, dim):
    return lax.broadcasted_iota(jnp.int32, shape, dim)


def shifted(u, reach, axis, first, last):
    size = u.shape[axis]
    place = iota(u.shape, axis)
    low = jnp.where(place >= first + reach, pltpu.roll(u, reach, axis), 0.0)
    high = jnp.where(place <= last - reach, pltpu.roll(u, size - reach, axis), 0.0)
    return low + high


def plane_pair(u, reach):
    return shifted(u, reach, 0, 0, NY - 1) + shifted(u, reach, 1, 0, NZ - 1)


def beside_fine(ref, p):
    u = ref[p]
    return u, ref[p - 1] + ref[p + 1] + plane_pair(u, 1)


def beside_mid(ref):
    u = ref[1 : SLABS + 1]
    lane = iota(u.shape, 2)
    inner = lane % 64
    across = jnp.where(lane < 64, ref[2 : SLABS + 2], ref[0:SLABS])
    total = pltpu.roll(u + across, 64, 2)
    total = total + shifted(u, 1, 1, 0, Y1 - 1)
    total = total + jnp.where(inner >= 1, pltpu.roll(u, 1, 2), 0.0)
    total = total + jnp.where(inner <= 62, pltpu.roll(u, 127, 2), 0.0)
    return u, total


def beside_low(ref):
    u = ref[1 : SLABS + 1]
    total = ref[2 : SLABS + 2] + ref[0:SLABS]
    total = total + shifted(u, 1, 1, 0, Y2 - 1) + shifted(u, 1, 2, 0, 31)
    return u, total


def kernel(
    psi_in, occ, ext, control, psi_out, hartree_out,
    psi, t1, t2, t3, pot, part, ringpart, half, d1, d2, f, va, vb, c1, m_a, m_b, l_a, l_b, mask1, mask2,
    tmp_res, tmp_mid, tmp_low, up, send, recv, local_sem,
):
    o = lax.axis_index("orb")
    d = lax.axis_index("dom")
    x = lax.rem(d, RING)
    g = lax.div(d, RING)

    barrier = pltpu.get_barrier_semaphore()
    for k in range(1, REACH + 1):
        for to in (lax.rem(d + k, DOM), lax.rem(d + DOM - k, DOM)):
            pl.semaphore_signal(barrier, inc=1, device_id={"orb": o, "dom": to})
    for k in range(1, ORB):
        pl.semaphore_signal(barrier, inc=1, device_id={"orb": lax.rem(o + k, ORB), "dom": d})

    own = pltpu.make_async_copy(
        psi_in.at[:, x], psi.at[0, :, pl.ds(WIDE + SLAB * x, SLAB)], local_sem.at[0]
    )
    own.start()

    def weight(b):
        return occ[b].astype(jnp.float32) * (1.0 / 16.0)

    for p in range(SLAB):
        total = jnp.zeros((NY, NZ), jnp.float32)
        for b in range(4):
            re, im = psi_in[0, b, p], psi_in[1, b, p]
            total = total + weight(b) * (re * re + im * im)
        part[0, p] = total

    for s in range(SLABS):
        inside = jnp.logical_and(d - REACH + s >= 0, d - REACH + s < DOM)
        factor = jnp.where(inside, 1.0, 0.0).astype(jnp.float32)
        mask1[s] = jnp.full((Y1, NZ), 1.0, jnp.float32) * factor
        mask2[s] = jnp.full((Y2, NZ), 1.0, jnp.float32) * factor
    for ref in (m_a, m_b, l_a, l_b):
        ref[0] = jnp.zeros(ref.shape[1:], jnp.float32)
        ref[SLABS + 1] = jnp.zeros(ref.shape[1:], jnp.float32)

    def clear_fine(p, carry):
        va[p] = jnp.zeros((NY, NZ), jnp.float32)
        vb[p] = jnp.zeros((NY, NZ), jnp.float32)
        return carry

    lax.fori_loop(0, FEXT, clear_fine, 0)

    def clear_halo(begin, refs):
        def body(p, carry):
            for ref in refs:
                for c in range(2):
                    ref[c, p] = jnp.zeros((NY, NZ), jnp.float32)
            return carry

        lax.fori_loop(begin, begin + WIDE, body, 0)

    @pl.when(g == 0)
    def _():
        clear_halo(0, (t1, t2, t3))

    @pl.when(g == GROUPS - 1)
    def _():
        clear_halo(WIDE + GROUP, (t1, t2, t3))

    pl.semaphore_wait(barrier, 2 * REACH + ORB - 1)

    pending = []

    def push(src, dst, orb, dom):
        i = len(pending)
        copy = pltpu.make_async_remote_copy(
            src_ref=src,
            dst_ref=dst,
            send_sem=send.at[i],
            recv_sem=recv.at[i],
            device_id={"orb": orb, "dom": dom},
            device_id_type=pl.DeviceIdType.MESH,
        )
        copy.start()
        pending.append(copy)
        return copy

    def mate(k):
        return lax.rem(x + k, RING)

    upper = x >= RING // 2
    beyond = lax.rem(g + jnp.where(upper, 1, GROUPS - 1), GROUPS)
    beyond_at = jnp.where(upper, SLAB * (x - RING // 2), WIDE + GROUP + SLAB * x)
    group_at = WIDE + SLAB * x

    row, col = iota((2 * NZ, NZ), 0), iota((2 * NZ, NZ), 1)
    down_fine = jnp.where(row // 2 == col, 0.125, 0.0).astype(jnp.float32)
    row, col = iota((NZ, NZ), 0), iota((NZ, NZ), 1)
    down_mid = jnp.where((row % 64) // 2 == col, 0.125, 0.0).astype(jnp.float32)
    up_low = jnp.where(row == (col % 64) // 2, 1.0, 0.0).astype(jnp.float32)
    row, col = iota((NZ, 2 * NZ), 0), iota((NZ, 2 * NZ), 1)
    up_mid = jnp.where(row == col // 2, 1.0, 0.0).astype(jnp.float32)

    def fine_range(lo, hi, body):
        begin = jnp.maximum(lo, WIDE - SLAB * d)
        end = jnp.minimum(hi, WIDE + NX - SLAB * d)

        def run(p, carry):
            body(p)
            return carry

        lax.fori_loop(begin, end, run, 0)

    def sweep_fine(step, src, dst, lo, hi):
        def body(p):
            u, beside = beside_fine(src, p)
            dst[p] = KEEP * u + RELAX * (f[step, p] + beside)

        fine_range(lo, hi, body)

    def coarse_source(step, cycle, v):
        sides = []
        for pair in range(2):
            total = None
            for p in (WIDE + 2 * pair, WIDE + 2 * pair + 1):
                u, beside = beside_fine(v, p)
                r = f[step, p] - (6.0 * u - beside)
                total = r if total is None else total + r
            sides.append(total)
        tmp_res[...] = dot(jnp.concatenate(sides, axis=1), down_fine)
        c1[step, cycle, REACH] = tmp_res[pl.ds(0, Y1, 2)] + tmp_res[pl.ds(1, Y1, 2)]
        copies = []
        reach = REACH if cycle == 0 else REACH - 1
        for k in range(1, reach + 1):
            src = c1.at[step, cycle, REACH]
            copies.append(push(src, c1.at[step, cycle, REACH - k], o, lax.rem(d + k, DOM)))
            copies.append(push(src, c1.at[step, cycle, REACH + k], o, lax.rem(d + DOM - k, DOM)))
        return copies

    def coarse_solve(step, cycle, lo, hi):
        if cycle == 1:
            c1[step, cycle, 0] = jnp.zeros((Y1, NZ), jnp.float32)
            c1[step, cycle, SLABS - 1] = jnp.zeros((Y1, NZ), jnp.float32)
        mid = slice(1, SLABS + 1)

        def source():
            return c1[step, cycle]

        def sweep(src, dst):
            u, beside = beside_mid(src)
            dst[mid] = (KEEP * u + RELAX * (4.0 * source() + beside)) * mask1[...]

        m_a[mid] = (4.0 * RELAX) * source() * mask1[...]
        sweep(m_a, m_b)
        u, beside = beside_mid(m_b)
        r = source() - 0.25 * (6.0 * u - beside)
        tmp_mid[...] = dot(r.reshape(SLABS * Y1, NZ), down_mid)
        low = tmp_mid[pl.ds(0, SLABS * Y2, 2)] + tmp_mid[pl.ds(1, SLABS * Y2, 2)]
        tmp_low[...] = low.reshape(SLABS, Y2, NZ)
        l_a[mid] = (16.0 * RELAX) * tmp_low[...] * mask2[...]
        src, dst = l_a, l_b
        for unused in range(3):
            u, beside = beside_low(src)
            dst[mid] = (KEEP * u + RELAX * (16.0 * tmp_low[...] + beside)) * mask2[...]
            src, dst = dst, src
        wide = dot(src[mid].reshape(SLABS * Y2, NZ), up_low)
        tmp_mid[pl.ds(0, SLABS * Y2, 2)] = wide
        tmp_mid[pl.ds(1, SLABS * Y2, 2)] = wide
        m_a[mid] = m_b[mid] + tmp_mid[...].reshape(SLABS, Y1, NZ)
        sweep(m_a, m_b)
        sweep(m_b, m_a)
        count = hi - lo
        fine = dot(m_a[1 + lo : 1 + hi].reshape(count * Y1, NZ), up_mid)
        for j in range(count):
            for side in range(2):
                piece = fine[j * Y1 : (j + 1) * Y1, side * NZ : (side + 1) * NZ]
                up[2 * j + side, pl.ds(0, Y1, 2)] = piece
                up[2 * j + side, pl.ds(1, Y1, 2)] = piece

    def add_up(v, lo, hi, base):
        def body(p):
            v[p] = v[p] + up[(p - base) // 2]

        fine_range(lo, hi, body)

    def solve(step):
        swap = push(part.at[step], d1.at[step], o + 1 - 2 * lax.rem(o, 2), d)
        swap.wait_recv()
        for p in range(SLAB):
            half[step, p] = part[step, p] + d1[step, p]
        swap = push(half.at[step], d2.at[step], lax.rem(o + 2, ORB), d)
        swap.wait_recv()
        for p in range(SLAB):
            f[step, WIDE + p] = COUPLING * (half[step, p] + d2[step, p])

        after = [lax.rem(d + k, DOM) for k in (1, 2)]
        before = [lax.rem(d + DOM - k, DOM) for k in (1, 2)]
        fs = f.at[step]
        near = [
            push(fs.at[pl.ds(WIDE + 2, 2)], fs.at[pl.ds(WIDE - 2, 2)], o, after[0]),
            push(fs.at[pl.ds(WIDE, 2)], fs.at[pl.ds(WIDE + SLAB, 2)], o, before[0]),
        ]
        far = [
            push(fs.at[pl.ds(WIDE, 2)], fs.at[pl.ds(WIDE - 4, 2)], o, after[0]),
            push(fs.at[pl.ds(WIDE + 2, 2)], fs.at[pl.ds(WIDE + SLAB + 2, 2)], o, before[0]),
            push(fs.at[pl.ds(WIDE, 4)], fs.at[pl.ds(WIDE - 8, 4)], o, after[1]),
            push(fs.at[pl.ds(WIDE, 4)], fs.at[pl.ds(WIDE + SLAB + 4, 4)], o, before[1]),
        ]

        def first(lo, hi):
            def body(p):
                va[p] = RELAX * f[step, p]

            fine_range(lo, hi, body)

        for copy in near:
            copy.wait_recv()
        first(6, 14)
        sweep_fine(step, va, vb, 7, 13)
        copies = coarse_source(step, 0, vb)
        for copy in far:
            copy.wait_recv()
        first(1, 6)
        first(14, 19)
        sweep_fine(step, va, vb, 2, 7)
        sweep_fine(step, va, vb, 13, 18)
        for copy in copies:
            copy.wait_recv()
        coarse_solve(step, 0, REACH - 2, REACH + 3)
        add_up(vb, 2, 18, 0)
        sweep_fine(step, vb, va, 3, 17)
        sweep_fine(step, va, vb, 4, 16)
        sweep_fine(step, vb, va, 5, 15)
        sweep_fine(step, va, vb, 6, 14)
        copies = coarse_source(step, 1, vb)
        for copy in copies:
            copy.wait_recv()
        coarse_solve(step, 1, REACH - 1, REACH + 2)
        add_up(vb, 6, 14, 4)
        sweep_fine(step, vb, va, 7, 13)
        sweep_fine(step, va, vb, 8, 12)

    def spread_potential(step):
        for p in range(SLAB):
            place = (SLAB * d + p).astype(jnp.float32)
            dipole = (place + 0.5) * (2.0 / NX) - 1.0
            pot[step, group_at + p] = ext[p] + vb[WIDE + p] + control[step] * dipole
        src = pot.at[step, pl.ds(group_at, SLAB)]
        copies = []
        for k in range(RING):
            copies.append(
                push(src, pot.at[step, pl.ds(beyond_at, SLAB)], o, RING * beyond + mate(k))
            )
        for k in range(1, RING):
            copies.append(push(src, src, o, RING * g + mate(k)))
        return copies

    def image(src, c, p, full):
        u = src[c, p]
        near = src[c, p - 1] + src[c, p + 1] + plane_pair(u, 1)
        far = src[c, p - 2] + src[c, p + 2] + plane_pair(u, 2)
        return full * u - (2.0 / 3.0) * near + (1.0 / 24.0) * far

    def group_range(lo, hi, body):
        begin = jnp.maximum(lo, WIDE - GROUP * g)
        end = jnp.minimum(hi, WIDE + NX - GROUP * g)

        def run(p, carry):
            body(p)
            return carry

        lax.fori_loop(begin, end, run, 0)

    def propagate(step):
        now = psi.at[step]
        for order, (src, dst) in enumerate(((now, t1), (t1, t2), (t2, t3)), 1):
            factor = TIME_STEP / order

            def body(p):
                full = pot[step, p] + 3.75
                dst[0, p] = factor * image(src, 1, p, full)
                dst[1, p] = -factor * image(src, 0, p, full)

            group_range(2 * order, EXT - 2 * order, body)
        factor = TIME_STEP / TERMS

        def last(p):
            full = pot[step, p] + 3.75
            re = factor * image(t3, 1, p, full)
            im = -factor * image(t3, 0, p, full)
            psi[step + 1, 0, p] = psi[step, 0, p] + t1[0, p] + t2[0, p] + t3[0, p] + re
            psi[step + 1, 1, p] = psi[step, 1, p] + t1[1, p] + t2[1, p] + t3[1, p] + im

        group_range(2 * TERMS, EXT - 2 * TERMS, last)

    moves = []
    for k in range(RING):
        to = mate(k)
        moves.append(
            push(
                psi_in.at[:, to],
                psi.at[0, :, pl.ds(beyond_at, SLAB)],
                o,
                RING * beyond + to,
            )
        )
    for k in range(1, RING):
        to = mate(k)
        moves.append(
            push(psi_in.at[:, to], psi.at[0, :, pl.ds(group_at, SLAB)], o, RING * g + to)
        )

    for step in range(STEPS):
        solve(step)
        spread = spread_potential(step)
        for copy in moves:
            copy.wait_recv()
        if step == 0:
            own.wait()

        @pl.when(g == 0)
        def _():
            clear_halo(0, (psi.at[step],))

        @pl.when(g == GROUPS - 1)
        def _():
            clear_halo(WIDE + GROUP, (psi.at[step],))

        for copy in spread:
            copy.wait_recv()
        propagate(step)
        if step == STEPS - 1:
            break
        later = psi.at[step + 1]

        def density(p, carry):
            re, im = psi[step + 1, 0, WIDE + p], psi[step + 1, 1, WIDE + p]
            ringpart[p] = weight(x) * (re * re + im * im)
            return carry

        lax.fori_loop(0, GROUP, density, 0)
        shares = []
        for k in range(1, RING):
            to = mate(k)
            shares.append(
                push(ringpart.at[pl.ds(SLAB * to, SLAB)], ringpart.at[pl.ds(GROUP + SLAB * (k - 1), SLAB)], o, RING * g + to)
            )
        for copy in shares:
            copy.wait_recv()
        for p in range(SLAB):
            total = ringpart[SLAB * x + p]
            for k in range(1, RING):
                total = total + ringpart[GROUP + SLAB * (k - 1) + p]
            part[step + 1, p] = total
        moves = [
            push(
                later.at[:, pl.ds(GROUP, WIDE)],
                later.at[:, pl.ds(0, WIDE)],
                o,
                lax.rem(d + RING, DOM),
            ),
            push(
                later.at[:, pl.ds(WIDE, WIDE)],
                later.at[:, pl.ds(WIDE + GROUP, WIDE)],
                o,
                lax.rem(d + DOM - RING, DOM),
            ),
        ]

    hartree_out[...] = vb[WIDE : WIDE + SLAB]
    final = psi.at[STEPS]
    own = pltpu.make_async_copy(
        final.at[:, pl.ds(group_at, SLAB)], psi_out.at[:, x], local_sem.at[1]
    )
    own.start()
    moves = []
    for k in range(1, RING):
        to = mate(k)
        moves.append(
            push(
                final.at[:, pl.ds(WIDE + SLAB * to, SLAB)], psi_out.at[:, x], o, RING * g + to
            )
        )
    for copy in moves:
        copy.wait_recv()
    own.wait()
    for copy in pending:
        copy.wait_send()


def per_device(orbitals, occupations, external, control):
    f32 = jnp.float32
    vmem = pl.BlockSpec(memory_space=pltpu.VMEM)
    smem = pl.BlockSpec(memory_space=pltpu.SMEM)
    fields = pltpu.VMEM((2, EXT, NY, NZ), f32)
    slab = pltpu.VMEM((STEPS, SLAB, NY, NZ), f32)
    mid = pltpu.VMEM((SLABS + 2, Y1, NZ), f32)
    low = pltpu.VMEM((SLABS + 2, Y2, NZ), f32)
    return pl.pallas_call(
        kernel,
        out_shape=(
            jax.ShapeDtypeStruct(orbitals.shape, f32),
            jax.ShapeDtypeStruct(external.shape, f32),
        ),
        in_specs=[vmem, smem, vmem, smem],
        out_specs=(pl.BlockSpec(memory_space=pl.ANY), vmem),
        scratch_shapes=[
            pltpu.VMEM((STEPS + 1, 2, EXT, NY, NZ), f32),
            fields, fields, fields,
            pltpu.VMEM((STEPS, EXT, NY, NZ), f32),
            slab,
            pltpu.VMEM((GROUP + SLAB * (RING - 1), NY, NZ), f32),
            slab, slab, slab,
            pltpu.VMEM((STEPS, FEXT, NY, NZ), f32),
            pltpu.VMEM((FEXT, NY, NZ), f32),
            pltpu.VMEM((FEXT, NY, NZ), f32),
            pltpu.VMEM((STEPS, 2, SLABS, Y1, NZ), f32),
            mid, mid, low, low,
            pltpu.VMEM((SLABS, Y1, NZ), f32),
            pltpu.VMEM((SLABS, Y2, NZ), f32),
            pltpu.VMEM((NY, NZ), f32),
            pltpu.VMEM((SLABS * Y1, NZ), f32),
            pltpu.VMEM((SLABS, Y2, NZ), f32),
            pltpu.VMEM((10, NY, NZ), f32),
            pltpu.SemaphoreType.DMA((COPIES,)),
            pltpu.SemaphoreType.DMA((COPIES,)),
            pltpu.SemaphoreType.DMA((2,)),
        ],
        compiler_params=pltpu.CompilerParams(
            collective_id=0, has_side_effects=True, vmem_limit_bytes=56 * 1024 * 1024
        ),
    )(orbitals, occupations, external, control)


def solution(mesh):
    in_specs = (P(None, "orb", "dom", None, None), P("orb"), P("dom", None, None), P())
    out_specs = (P(None, "orb", "dom", None, None), P("dom", None, None))
    return jax.shard_map(
        per_device, mesh=mesh, in_specs=in_specs, out_specs=out_specs, check_vma=False
    )
```

time: 1100 us -> 259 us (0.24); the launches traced: 1090 us -> 256 us
  starting transfers between devices: 705 us -> 0 us
  Pallas kernels: 0 us -> 252 us
  waiting for transfers between devices: 244 us -> 0 us
  local copies, waits for them, and re-layouts: 64.8 us -> 3 us
  other arithmetic: 54.8 us -> 0 us
  between operations: 16.8 us -> 0.65 us
    ppermute x114 -> x0, starting transfers between devices: 705 us -> none  [the longest x57 592 us: with_halo(): lax.ppermute(lax.slice_in_dim(block, block.shape[dim] - width, None, axis...]
    pallas_call x0 -> x1, Pallas kernels: none -> 252 us  [per_device(): pl.pallas_call(kernel, out_shape=(jax.ShapeDtypeStruct(orbitals.shape, f3...]
    ppermute x114 -> x0, waiting for transfers between devices: 172 us -> none  [the longest x57 112 us: with_halo(): lax.ppermute(lax.slice_in_dim(block, 0, width, axis=dim), axis, backward)]
    psum x2 -> x0, waiting for transfers between devices: 71.8 us -> none  [per_device(): source = coupling * lax.psum(local, 'orb')]
    reshape x12 -> x0, local copies, waits for them, and re-layouts: 47.1 us -> none  [the longest x4 39.9 us: restrict(): return field.reshape(a // 2, 2, b // 2, 2, c // 2, 2).mean(axis=(1, 3, 5))]
    reduce_sum x14 -> x0, other arithmetic: 21.9 us -> none  [the longest x12 19.2 us: restrict(): return field.reshape(a // 2, 2, b // 2, 2, c // 2, 2).mean(axis=(1, 3, 5))]
    add x56 -> x0, other arithmetic: 21.7 us -> none  [the longest x8 9.9 us: shrink_apply(): return -0.5 * laplace + potential * center]
  transfers between devices with their start and end apart: 116 -> 0, of which waited for: 60 -> 0; matrix products, arithmetic and copies ran while one was open for 2% -> 0% of each run, Pallas kernels for 0% -> 0%
where the time goes in v1:
time: 259 us; the launch traced here: 256 us
  Pallas kernels  252 us (97%)
  local copies, waits for them, and re-layouts  3 us (1%)
    pallas_call x1, Pallas kernels, per_device(): pl.pallas_call(kernel, out_shape=(jax.ShapeDtypeStruct(orbitals.shape, f3...  252 us

profile of v1, /device:TPU:94, one launch (start us, length us, event | category | flops | bytes accessed | tf_op | source)
XLA Modules:
  0.0 255.7 jit_solution(3426742346974347362)
XLA Ops:
  0.6 252.1 %shard_map.59 = (f32[2,4,4,64,128]{4,3,2,1,0:T(8,128)}, f32[4,64,128]{2,1,0:T(8,128)}) custom-call(f32[2,4,4,64,128]{4,3,2,1,0:T(8,128)} %psi_in.1, s32[4]{0:T(128)} %occ.1, f32[4,64,128]{2,1,0:T(8,128)} %ext.1, f32[2]{0:T(128)} %control.1), custom_call_target="tpu_custom_call" | custom-call | tf_op jit(solution)/shard_map/pallas_call | solution.py:473
  252.7 0.0 copy-start
  252.7 2.3 copy.8
  255.1 0.0 copy-done
  255.1 0.7 copy.9
Async XLA Ops:
  252.7 2.4 copy-start

commit v2 on v1

--- a/solution.py
+++ b/solution.py
@@ -162,9 +162,7 @@
     def mate(k):
         return lax.rem(x + k, RING)
 
-    upper = x >= RING // 2
-    beyond = lax.rem(g + jnp.where(upper, 1, GROUPS - 1), GROUPS)
-    beyond_at = jnp.where(upper, SLAB * (x - RING // 2), WIDE + GROUP + SLAB * x)
+    after_group, before_group = lax.rem(d + RING, DOM), lax.rem(d + DOM - RING, DOM)
     group_at = WIDE + SLAB * x
 
     row, col = iota((2 * NZ, NZ), 0), iota((2 * NZ, NZ), 1)
@@ -257,7 +255,7 @@
 
         fine_range(lo, hi, body)
 
-    def solve(step):
+    def solve(step, meanwhile):
         swap = push(part.at[step], d1.at[step], o + 1 - 2 * lax.rem(o, 2), d)
         swap.wait_recv()
         for p in range(SLAB):
@@ -292,6 +290,7 @@
         first(6, 14)
         sweep_fine(step, va, vb, 7, 13)
         copies = coarse_source(step, 0, vb)
+        meanwhile()
         for copy in far:
             copy.wait_recv()
         first(1, 6)
@@ -320,14 +319,22 @@
             dipole = (place + 0.5) * (2.0 / NX) - 1.0
             pot[step, group_at + p] = ext[p] + vb[WIDE + p] + control[step] * dipole
         src = pot.at[step, pl.ds(group_at, SLAB)]
-        copies = []
-        for k in range(RING):
-            copies.append(
-                push(src, pot.at[step, pl.ds(beyond_at, SLAB)], o, RING * beyond + mate(k))
-            )
-        for k in range(1, RING):
-            copies.append(push(src, src, o, RING * g + mate(k)))
-        return copies
+        return [push(src, src, o, RING * g + mate(k)) for k in range(1, RING)]
+
+    def spread_halo(step):
+        at = pot.at[step]
+        return [
+            push(at.at[pl.ds(WIDE + GROUP - 6, 6)], at.at[pl.ds(WIDE - 6, 6)], o, after_group),
+            push(at.at[pl.ds(WIDE, 6)], at.at[pl.ds(WIDE + GROUP, 6)], o, before_group),
+        ]
+
+    def low_halo(ref):
+        return push(ref.at[:, pl.ds(GROUP, WIDE)], ref.at[:, pl.ds(0, WIDE)], o, after_group)
+
+    def high_halo(ref):
+        return push(
+            ref.at[:, pl.ds(WIDE, WIDE)], ref.at[:, pl.ds(WIDE + GROUP, WIDE)], o, before_group
+        )
 
     def image(src, c, p, full):
         u = src[c, p]
@@ -345,52 +352,87 @@
 
         lax.fori_loop(begin, end, run, 0)
 
-    def propagate(step):
-        now = psi.at[step]
-        for order, (src, dst) in enumerate(((now, t1), (t1, t2), (t2, t3)), 1):
-            factor = TIME_STEP / order
-
-            def body(p):
-                full = pot[step, p] + 3.75
-                dst[0, p] = factor * image(src, 1, p, full)
-                dst[1, p] = -factor * image(src, 0, p, full)
-
-            group_range(2 * order, EXT - 2 * order, body)
-        factor = TIME_STEP / TERMS
-
-        def last(p):
+    def term(step, order, lo, hi):
+        src, dst = ((psi.at[step], t1), (t1, t2), (t2, t3), (t3, None))[order - 1]
+        factor = TIME_STEP / order
+
+        def body(p):
             full = pot[step, p] + 3.75
-            re = factor * image(t3, 1, p, full)
-            im = -factor * image(t3, 0, p, full)
-            psi[step + 1, 0, p] = psi[step, 0, p] + t1[0, p] + t2[0, p] + t3[0, p] + re
-            psi[step + 1, 1, p] = psi[step, 1, p] + t1[1, p] + t2[1, p] + t3[1, p] + im
-
-        group_range(2 * TERMS, EXT - 2 * TERMS, last)
-
-    moves = []
-    for k in range(RING):
-        to = mate(k)
-        moves.append(
-            push(
-                psi_in.at[:, to],
-                psi.at[0, :, pl.ds(beyond_at, SLAB)],
-                o,
-                RING * beyond + to,
-            )
-        )
+            re = factor * image(src, 1, p, full)
+            im = -factor * image(src, 0, p, full)
+            if order < TERMS:
+                dst[0, p] = re
+                dst[1, p] = im
+                return
+            re = re + (psi[step, 0, p] + t1[0, p]) + (t2[0, p] + t3[0, p])
+            im = im + (psi[step, 1, p] + t1[1, p]) + (t2[1, p] + t3[1, p])
+            psi[step + 1, 0, p] = re
+            psi[step + 1, 1, p] = im
+            if step < STEPS - 1:
+                ringpart[p - WIDE] = weight(x) * (re * re + im * im)
+
+        group_range(lo, hi, body)
+
+    def inside(step):
+        for order in range(1, TERMS + 1):
+            cut = 2 * (order - 1)
+            term(step, order, WIDE + cut, WIDE + GROUP - cut)
+
+    def low_edge(step):
+        for order in range(1, TERMS + 1):
+            term(step, order, 2 * order, 2 * order + 6)
+
+    def high_edge(step):
+        for order in range(1, TERMS + 1):
+            term(step, order, EXT - 6 - 2 * order, EXT - 2 * order)
+
+    class Shares:
+        def __init__(self, src_of, dst_of):
+            self.copies = []
+            for k in range(1, RING):
+                to = mate(k)
+                i = len(pending)
+                copy = pltpu.make_async_remote_copy(
+                    src_ref=src_of(to),
+                    dst_ref=dst_of(k),
+                    send_sem=send.at[i],
+                    recv_sem=recv.at[i],
+                    device_id={"orb": o, "dom": RING * g + to},
+                    device_id_type=pl.DeviceIdType.MESH,
+                )
+                pending.append(copy)
+                self.copies.append((to, copy))
+
+        def begin(self, lo, hi):
+            for to, copy in self.copies:
+                pl.when(jnp.logical_and(to >= lo, to < hi))(copy.start)
+
+        def wait(self):
+            for unused, copy in self.copies:
+                copy.wait_recv()
+
+    regroup = []
     for k in range(1, RING):
         to = mate(k)
-        moves.append(
+        regroup.append(
             push(psi_in.at[:, to], psi.at[0, :, pl.ds(group_at, SLAB)], o, RING * g + to)
         )
+    halos = []
+
+    def regrouped():
+        for copy in regroup:
+            copy.wait_recv()
+        own.wait()
+        halos.append(low_halo(psi.at[0]))
+        halos.append(high_halo(psi.at[0]))
 
     for step in range(STEPS):
-        solve(step)
-        spread = spread_potential(step)
-        for copy in moves:
-            copy.wait_recv()
-        if step == 0:
-            own.wait()
+        solve(step, regrouped if step == 0 else lambda: None)
+        for copy in spread_potential(step):
+            copy.wait_recv()
+        spread = spread_halo(step)
+        for copy in halos:
+            copy.wait_recv()
 
         @pl.when(g == 0)
         def _():
@@ -400,46 +442,34 @@
         def _():
             clear_halo(WIDE + GROUP, (psi.at[step],))
 
+        inside(step)
         for copy in spread:
             copy.wait_recv()
-        propagate(step)
-        if step == STEPS - 1:
-            break
         later = psi.at[step + 1]
-
-        def density(p, carry):
-            re, im = psi[step + 1, 0, WIDE + p], psi[step + 1, 1, WIDE + p]
-            ringpart[p] = weight(x) * (re * re + im * im)
-            return carry
-
-        lax.fori_loop(0, GROUP, density, 0)
-        shares = []
-        for k in range(1, RING):
-            to = mate(k)
-            shares.append(
-                push(ringpart.at[pl.ds(SLAB * to, SLAB)], ringpart.at[pl.ds(GROUP + SLAB * (k - 1), SLAB)], o, RING * g + to)
+        if step < STEPS - 1:
+            shares = Shares(
+                lambda to: ringpart.at[pl.ds(SLAB * to, SLAB)],
+                lambda k: ringpart.at[pl.ds(GROUP + SLAB * (k - 1), SLAB)],
             )
-        for copy in shares:
-            copy.wait_recv()
-        for p in range(SLAB):
-            total = ringpart[SLAB * x + p]
-            for k in range(1, RING):
-                total = total + ringpart[GROUP + SLAB * (k - 1) + p]
-            part[step + 1, p] = total
-        moves = [
-            push(
-                later.at[:, pl.ds(GROUP, WIDE)],
-                later.at[:, pl.ds(0, WIDE)],
-                o,
-                lax.rem(d + RING, DOM),
-            ),
-            push(
-                later.at[:, pl.ds(WIDE, WIDE)],
-                later.at[:, pl.ds(WIDE + GROUP, WIDE)],
-                o,
-                lax.rem(d + DOM - RING, DOM),
-            ),
-        ]
+        else:
+            shares = Shares(
+                lambda to: later.at[:, pl.ds(WIDE + SLAB * to, SLAB)],
+                lambda k: psi_out.at[:, x],
+            )
+        low_edge(step)
+        shares.begin(0, RING // 2)
+        if step < STEPS - 1:
+            halos = [high_halo(later)]
+        high_edge(step)
+        shares.begin(RING // 2, RING)
+        if step < STEPS - 1:
+            halos.append(low_halo(later))
+            shares.wait()
+            for p in range(SLAB):
+                total = ringpart[SLAB * x + p]
+                for k in range(1, RING):
+                    total = total + ringpart[GROUP + SLAB * (k - 1) + p]
+                part[step + 1, p] = total
 
     hartree_out[...] = vb[WIDE : WIDE + SLAB]
     final = psi.at[STEPS]
@@ -447,16 +477,7 @@
         final.at[:, pl.ds(group_at, SLAB)], psi_out.at[:, x], local_sem.at[1]
     )
     own.start()
-    moves = []
-    for k in range(1, RING):
-        to = mate(k)
-        moves.append(
-            push(
-                final.at[:, pl.ds(WIDE + SLAB * to, SLAB)], psi_out.at[:, x], o, RING * g + to
-            )
-        )
-    for copy in moves:
-        copy.wait_recv()
+    shares.wait()
     own.wait()
     for copy in pending:
         copy.wait_send()

time: 259 us -> 187 us (0.72)
  the two profiles are of different devices: /device:TPU:94 before, /device:TPU:68 now
where the time goes in v2:
time: 187 us
  Pallas kernels  183 us (98%)
  local copies, waits for them, and re-layouts  3 us (2%)
    pallas_call x1, Pallas kernels, per_device(): pl.pallas_call(kernel, out_shape=(jax.ShapeDtypeStruct(orbitals.shape, f3...  183 us

profile of v2, /device:TPU:68, one launch (start us, length us, event | category | flops | bytes accessed | tf_op | source)
XLA Modules:
  0.0 186.9 jit_solution(2821183950427735700)
XLA Ops:
  0.6 183.3 %shard_map.59 = (f32[2,4,4,64,128]{4,3,2,1,0:T(8,128)}, f32[4,64,128]{2,1,0:T(8,128)}) custom-call(f32[2,4,4,64,128]{4,3,2,1,0:T(8,128)} %psi_in.1, s32[4]{0:T(128)} %occ.1, f32[4,64,128]{2,1,0:T(8,128)} %ext.1, f32[2]{0:T(128)} %control.1), custom_call_target="tpu_custom_call" | custom-call | tf_op jit(solution)/shard_map/pallas_call | solution.py:494
  183.9 0.0 copy-start
  183.9 2.3 %copy.8 = f32[2,4,4,64,128]{4,3,2,1,0:T(8,128)} copy(f32[2,4,4,64,128]{4,3,2,1,0:T(8,128)} %get-tuple-element.4) | data formatting | bytes 2097152
  186.3 0.0 copy-done
  186.3 0.7 copy.9
Async XLA Ops:
  183.9 2.4 %copy-start = (f32[4,64,128]{2,1,0:T(8,128)S(1)}, f32[4,64,128]{2,1,0:T(8,128)}, u32[]{:S(2)}) copy-start(f32[4,64,128]{2,1,0:T(8,128)} %get-tuple-element.5) | copy-start | bytes 393220

commit v3 on v2

--- a/solution.py
+++ b/solution.py
@@ -40,46 +40,84 @@
     return lax.broadcasted_iota(jnp.int32, shape, dim)
 
 
-def shifted(u, reach, axis, first, last):
-    size = u.shape[axis]
+def flipped(a, up):
+    axis = a.ndim - 2
+    place = iota(a.shape, axis)
+    if up:
+        return jnp.where(place <= 6, pltpu.roll(a, 7, axis), 0.0)
+    return jnp.where(place >= 1, pltpu.roll(a, 1, axis), 0.0)
+
+
+def rows(u, begin, count):
+    return u[..., 8 * begin : 8 * (begin + count), :]
+
+
+def y_pairs(u, reaches):
+    tiles = u.shape[-2] // 8
+    axis = u.ndim - 2
+    first = [flipped(rows(u, i, 1), True) for i in range(reaches)]
+    last = [flipped(rows(u, tiles - 1 - i, 1), False) for i in range(reaches)]
+    sums = []
+    for reach in range(1, reaches + 1):
+        up = jnp.concatenate([rows(u, reach, tiles - reach)] + first[:reach], axis=axis)
+        down = jnp.concatenate(last[:reach][::-1] + [rows(u, 0, tiles - reach)], axis=axis)
+        sums.append(up + down)
+    return sums
+
+
+def z_pair(u, reach, period=NZ):
+    axis = u.ndim - 1
     place = iota(u.shape, axis)
-    low = jnp.where(place >= first + reach, pltpu.roll(u, reach, axis), 0.0)
-    high = jnp.where(place <= last - reach, pltpu.roll(u, size - reach, axis), 0.0)
+    if period < NZ:
+        place = place % 64
+    low = jnp.where(place >= reach, pltpu.roll(u, reach, axis), 0.0)
+    high = jnp.where(place <= period - 1 - reach, pltpu.roll(u, NZ - reach, axis), 0.0)
     return low + high
-
-
-def plane_pair(u, reach):
-    return shifted(u, reach, 0, 0, NY - 1) + shifted(u, reach, 1, 0, NZ - 1)
 
 
 def beside_fine(ref, p):
     u = ref[p]
-    return u, ref[p - 1] + ref[p + 1] + plane_pair(u, 1)
+    return u, (ref[p - 1] + ref[p + 1]) + (y_pairs(u, 1)[0] + z_pair(u, 1))
 
 
 def beside_mid(ref):
     u = ref[1 : SLABS + 1]
     lane = iota(u.shape, 2)
-    inner = lane % 64
     across = jnp.where(lane < 64, ref[2 : SLABS + 2], ref[0:SLABS])
     total = pltpu.roll(u + across, 64, 2)
-    total = total + shifted(u, 1, 1, 0, Y1 - 1)
-    total = total + jnp.where(inner >= 1, pltpu.roll(u, 1, 2), 0.0)
-    total = total + jnp.where(inner <= 62, pltpu.roll(u, 127, 2), 0.0)
-    return u, total
+    return u, total + (y_pairs(u, 1)[0] + z_pair(u, 1, 64))
 
 
 def beside_low(ref):
     u = ref[1 : SLABS + 1]
     total = ref[2 : SLABS + 2] + ref[0:SLABS]
-    total = total + shifted(u, 1, 1, 0, Y2 - 1) + shifted(u, 1, 2, 0, 31)
-    return u, total
+    return u, total + (y_pairs(u, 1)[0] + z_pair(u, 1, 32))
+
+
+def halved(t):
+    tiles = t.shape[-2] // 8
+    pairs = [rows(t, 2 * i, 1) + rows(t, 2 * i + 1, 1) for i in range(tiles // 2)]
+    return jnp.concatenate(pairs, axis=t.ndim - 2)
+
+
+def doubled(t):
+    tiles = t.shape[-2] // 8
+    return jnp.concatenate([rows(t, i // 2, 1) for i in range(2 * tiles)], axis=t.ndim - 2)
+
+
+def gathered(ref, *at):
+    return jnp.concatenate([ref[(*at, pl.ds(v, 8, stride=8))] for v in range(8)], axis=0)
+
+
+def scatter(ref, value, *at):
+    for v in range(8):
+        ref[(*at, pl.ds(v, 8, stride=8))] = value[8 * v : 8 * v + 8]
 
 
 def kernel(
     psi_in, occ, ext, control, psi_out, hartree_out,
     psi, t1, t2, t3, pot, part, ringpart, half, d1, d2, f, va, vb, c1, m_a, m_b, l_a, l_b, mask1, mask2,
-    tmp_res, tmp_mid, tmp_low, up, send, recv, local_sem,
+    land, plane, tmp_low, up, send, recv, local_sem,
 ):
     o = lax.axis_index("orb")
     d = lax.axis_index("dom")
@@ -94,7 +132,7 @@
         pl.semaphore_signal(barrier, inc=1, device_id={"orb": lax.rem(o + k, ORB), "dom": d})
 
     own = pltpu.make_async_copy(
-        psi_in.at[:, x], psi.at[0, :, pl.ds(WIDE + SLAB * x, SLAB)], local_sem.at[0]
+        psi_in.at[:, x], land.at[:, pl.ds(SLAB * x, SLAB)], local_sem.at[0]
     )
     own.start()
 
@@ -106,7 +144,8 @@
         for b in range(4):
             re, im = psi_in[0, b, p], psi_in[1, b, p]
             total = total + weight(b) * (re * re + im * im)
-        part[0, p] = total
+        plane[p] = total
+        part[0, p] = gathered(plane, p)
 
     for s in range(SLABS):
         inside = jnp.logical_and(d - REACH + s >= 0, d - REACH + s < DOM)
@@ -124,22 +163,22 @@
 
     lax.fori_loop(0, FEXT, clear_fine, 0)
 
-    def clear_halo(begin, refs):
+    def clear_halo(begin, count, refs):
         def body(p, carry):
             for ref in refs:
                 for c in range(2):
                     ref[c, p] = jnp.zeros((NY, NZ), jnp.float32)
             return carry
 
-        lax.fori_loop(begin, begin + WIDE, body, 0)
+        lax.fori_loop(begin, begin + count, body, 0)
 
     @pl.when(g == 0)
     def _():
-        clear_halo(0, (t1, t2, t3))
+        clear_halo(0, WIDE, (t1, t2, t3))
 
     @pl.when(g == GROUPS - 1)
     def _():
-        clear_halo(WIDE + GROUP, (t1, t2, t3))
+        clear_halo(WIDE + GROUP, WIDE, (t1, t2, t3))
 
     pl.semaphore_wait(barrier, 2 * REACH + ORB - 1)
 
@@ -164,6 +203,8 @@
 
     after_group, before_group = lax.rem(d + RING, DOM), lax.rem(d + DOM - RING, DOM)
     group_at = WIDE + SLAB * x
+    core = lax.rem(o, 2)
+    sibling = o + 1 - 2 * core
 
     row, col = iota((2 * NZ, NZ), 0), iota((2 * NZ, NZ), 1)
     down_fine = jnp.where(row // 2 == col, 0.125, 0.0).astype(jnp.float32)
@@ -198,25 +239,37 @@
                 u, beside = beside_fine(v, p)
                 r = f[step, p] - (6.0 * u - beside)
                 total = r if total is None else total + r
-            sides.append(total)
-        tmp_res[...] = dot(jnp.concatenate(sides, axis=1), down_fine)
-        c1[step, cycle, REACH] = tmp_res[pl.ds(0, Y1, 2)] + tmp_res[pl.ds(1, Y1, 2)]
+            sides.append(halved(total))
+        c1[step, cycle, REACH] = dot(jnp.concatenate(sides, axis=1), down_fine).reshape(2, Y2, NZ)
         copies = []
         reach = REACH if cycle == 0 else REACH - 1
         for k in range(1, reach + 1):
-            src = c1.at[step, cycle, REACH]
-            copies.append(push(src, c1.at[step, cycle, REACH - k], o, lax.rem(d + k, DOM)))
-            copies.append(push(src, c1.at[step, cycle, REACH + k], o, lax.rem(d + DOM - k, DOM)))
+            src = c1.at[step, cycle, REACH, core]
+            low = c1.at[step, cycle, REACH - k, core]
+            high = c1.at[step, cycle, REACH + k, core]
+            copies.append(push(src, low, o, lax.rem(d + k, DOM)))
+            copies.append(push(src, high, o, lax.rem(d + DOM - k, DOM)))
         return copies
+
+    def whole_source(step, cycle, copies):
+        for copy in copies:
+            copy.wait_recv()
+        reach = len(copies) // 2
+        swaps = []
+        for begin in (REACH - reach, REACH + 1):
+            piece = c1.at[step, cycle, pl.ds(begin, reach), core]
+            swaps.append(push(piece, piece, sibling, d))
+        for copy in swaps:
+            copy.wait_recv()
 
     def coarse_solve(step, cycle, lo, hi):
         if cycle == 1:
-            c1[step, cycle, 0] = jnp.zeros((Y1, NZ), jnp.float32)
-            c1[step, cycle, SLABS - 1] = jnp.zeros((Y1, NZ), jnp.float32)
+            c1[step, cycle, 0] = jnp.zeros((2, Y2, NZ), jnp.float32)
+            c1[step, cycle, SLABS - 1] = jnp.zeros((2, Y2, NZ), jnp.float32)
         mid = slice(1, SLABS + 1)
 
         def source():
-            return c1[step, cycle]
+            return c1[step, cycle].reshape(SLABS, Y1, NZ)
 
         def sweep(src, dst):
             u, beside = beside_mid(src)
@@ -226,8 +279,7 @@
         sweep(m_a, m_b)
         u, beside = beside_mid(m_b)
         r = source() - 0.25 * (6.0 * u - beside)
-        tmp_mid[...] = dot(r.reshape(SLABS * Y1, NZ), down_mid)
-        low = tmp_mid[pl.ds(0, SLABS * Y2, 2)] + tmp_mid[pl.ds(1, SLABS * Y2, 2)]
+        low = dot(halved(r).reshape(SLABS * Y2, NZ), down_mid)
         tmp_low[...] = low.reshape(SLABS, Y2, NZ)
         l_a[mid] = (16.0 * RELAX) * tmp_low[...] * mask2[...]
         src, dst = l_a, l_b
@@ -236,9 +288,7 @@
             dst[mid] = (KEEP * u + RELAX * (16.0 * tmp_low[...] + beside)) * mask2[...]
             src, dst = dst, src
         wide = dot(src[mid].reshape(SLABS * Y2, NZ), up_low)
-        tmp_mid[pl.ds(0, SLABS * Y2, 2)] = wide
-        tmp_mid[pl.ds(1, SLABS * Y2, 2)] = wide
-        m_a[mid] = m_b[mid] + tmp_mid[...].reshape(SLABS, Y1, NZ)
+        m_a[mid] = m_b[mid] + doubled(wide.reshape(SLABS, Y2, NZ))
         sweep(m_a, m_b)
         sweep(m_b, m_a)
         count = hi - lo
@@ -246,8 +296,7 @@
         for j in range(count):
             for side in range(2):
                 piece = fine[j * Y1 : (j + 1) * Y1, side * NZ : (side + 1) * NZ]
-                up[2 * j + side, pl.ds(0, Y1, 2)] = piece
-                up[2 * j + side, pl.ds(1, Y1, 2)] = piece
+                up[2 * j + side] = doubled(piece)
 
     def add_up(v, lo, hi, base):
         def body(p):
@@ -256,7 +305,7 @@
         fine_range(lo, hi, body)
 
     def solve(step, meanwhile):
-        swap = push(part.at[step], d1.at[step], o + 1 - 2 * lax.rem(o, 2), d)
+        swap = push(part.at[step], d1.at[step], sibling, d)
         swap.wait_recv()
         for p in range(SLAB):
             half[step, p] = part[step, p] + d1[step, p]
@@ -265,6 +314,7 @@
         for p in range(SLAB):
             f[step, WIDE + p] = COUPLING * (half[step, p] + d2[step, p])
 
+        meanwhile('density')
         after = [lax.rem(d + k, DOM) for k in (1, 2)]
         before = [lax.rem(d + DOM - k, DOM) for k in (1, 2)]
         fs = f.at[step]
@@ -273,11 +323,13 @@
             push(fs.at[pl.ds(WIDE, 2)], fs.at[pl.ds(WIDE + SLAB, 2)], o, before[0]),
         ]
         far = [
-            push(fs.at[pl.ds(WIDE, 2)], fs.at[pl.ds(WIDE - 4, 2)], o, after[0]),
-            push(fs.at[pl.ds(WIDE + 2, 2)], fs.at[pl.ds(WIDE + SLAB + 2, 2)], o, before[0]),
-            push(fs.at[pl.ds(WIDE, 4)], fs.at[pl.ds(WIDE - 8, 4)], o, after[1]),
-            push(fs.at[pl.ds(WIDE, 4)], fs.at[pl.ds(WIDE + SLAB + 4, 4)], o, before[1]),
+            push(fs.at[pl.ds(WIDE + core, 1)], fs.at[pl.ds(WIDE - 4 + core, 1)], o, after[0]),
+            push(fs.at[pl.ds(WIDE + 2 + core, 1)], fs.at[pl.ds(14 + core, 1)], o, before[0]),
+            push(fs.at[pl.ds(WIDE + 2 * core, 2)], fs.at[pl.ds(2 * core, 2)], o, after[1]),
+            push(fs.at[pl.ds(WIDE + 2 * core, 2)], fs.at[pl.ds(16 + 2 * core, 2)], o, before[1]),
         ]
+
+        meanwhile('near')
 
         def first(lo, hi):
             def body(p):
@@ -290,15 +342,20 @@
         first(6, 14)
         sweep_fine(step, va, vb, 7, 13)
         copies = coarse_source(step, 0, vb)
-        meanwhile()
+        meanwhile('source')
+        for copy in far:
+            copy.wait_recv()
+        far = []
+        for at, count in ((4 + core, 1), (14 + core, 1), (2 * core, 2), (16 + 2 * core, 2)):
+            piece = fs.at[pl.ds(at, count)]
+            far.append(push(piece, piece, sibling, d))
         for copy in far:
             copy.wait_recv()
         first(1, 6)
         first(14, 19)
         sweep_fine(step, va, vb, 2, 7)
         sweep_fine(step, va, vb, 13, 18)
-        for copy in copies:
-            copy.wait_recv()
+        whole_source(step, 0, copies)
         coarse_solve(step, 0, REACH - 2, REACH + 3)
         add_up(vb, 2, 18, 0)
         sweep_fine(step, vb, va, 3, 17)
@@ -306,8 +363,9 @@
         sweep_fine(step, vb, va, 5, 15)
         sweep_fine(step, va, vb, 6, 14)
         copies = coarse_source(step, 1, vb)
-        for copy in copies:
-            copy.wait_recv()
+        meanwhile('again')
+        whole_source(step, 1, copies)
+        meanwhile('whole')
         coarse_solve(step, 1, REACH - 1, REACH + 2)
         add_up(vb, 6, 14, 4)
         sweep_fine(step, vb, va, 7, 13)
@@ -317,7 +375,7 @@
         for p in range(SLAB):
             place = (SLAB * d + p).astype(jnp.float32)
             dipole = (place + 0.5) * (2.0 / NX) - 1.0
-            pot[step, group_at + p] = ext[p] + vb[WIDE + p] + control[step] * dipole
+            pot[step, group_at + p] = gathered(ext, p) + vb[WIDE + p] + control[step] * dipole
         src = pot.at[step, pl.ds(group_at, SLAB)]
         return [push(src, src, o, RING * g + mate(k)) for k in range(1, RING)]
 
@@ -328,18 +386,29 @@
             push(at.at[pl.ds(WIDE, 6)], at.at[pl.ds(WIDE + GROUP, 6)], o, before_group),
         ]
 
-    def low_halo(ref):
-        return push(ref.at[:, pl.ds(GROUP, WIDE)], ref.at[:, pl.ds(0, WIDE)], o, after_group)
-
-    def high_halo(ref):
-        return push(
-            ref.at[:, pl.ds(WIDE, WIDE)], ref.at[:, pl.ds(WIDE + GROUP, WIDE)], o, before_group
-        )
+    def halo(step, begin, count):
+        ref = psi.at[step]
+        far = begin + count
+        return [
+            push(
+                ref.at[:, pl.ds(WIDE + GROUP - far, count)],
+                ref.at[:, pl.ds(WIDE - far, count)],
+                o,
+                after_group,
+            ),
+            push(
+                ref.at[:, pl.ds(WIDE + begin, count)],
+                ref.at[:, pl.ds(WIDE + GROUP + begin, count)],
+                o,
+                before_group,
+            ),
+        ]
 
     def image(src, c, p, full):
         u = src[c, p]
-        near = src[c, p - 1] + src[c, p + 1] + plane_pair(u, 1)
-        far = src[c, p - 2] + src[c, p + 2] + plane_pair(u, 2)
+        y_near, y_far = y_pairs(u, 2)
+        near = (src[c, p - 1] + src[c, p + 1]) + (y_near + z_pair(u, 1))
+        far = (src[c, p - 2] + src[c, p + 2]) + (y_far + z_pair(u, 2))
         return full * u - (2.0 / 3.0) * near + (1.0 / 24.0) * far
 
     def group_range(lo, hi, body):
@@ -347,10 +416,11 @@
         end = jnp.minimum(hi, WIDE + NX - GROUP * g)
 
         def run(p, carry):
-            body(p)
+            body(begin + 2 * p)
+            body(begin + 2 * p + 1)
             return carry
 
-        lax.fori_loop(begin, end, run, 0)
+        lax.fori_loop(0, (end - begin) // 2, run, 0)
 
     def term(step, order, lo, hi):
         src, dst = ((psi.at[step], t1), (t1, t2), (t2, t3), (t3, None))[order - 1]
@@ -366,9 +436,12 @@
                 return
             re = re + (psi[step, 0, p] + t1[0, p]) + (t2[0, p] + t3[0, p])
             im = im + (psi[step, 1, p] + t1[1, p]) + (t2[1, p] + t3[1, p])
-            psi[step + 1, 0, p] = re
-            psi[step + 1, 1, p] = im
-            if step < STEPS - 1:
+            if step == STEPS - 1:
+                scatter(psi, re, step + 1, 0, p)
+                scatter(psi, im, step + 1, 1, p)
+            else:
+                psi[step + 1, 0, p] = re
+                psi[step + 1, 1, p] = im
                 ringpart[p - WIDE] = weight(x) * (re * re + im * im)
 
         group_range(lo, hi, body)
@@ -412,37 +485,69 @@
                 copy.wait_recv()
 
     regroup = []
-    for k in range(1, RING):
-        to = mate(k)
-        regroup.append(
-            push(psi_in.at[:, to], psi.at[0, :, pl.ds(group_at, SLAB)], o, RING * g + to)
-        )
-    halos = []
+
+    def begin_regroup():
+        for k in range(1, RING):
+            to = mate(k)
+            regroup.append(
+                push(psi_in.at[:, to], land.at[:, pl.ds(SLAB * x, SLAB)], o, RING * g + to)
+            )
+
+    halos = {}
 
     def regrouped():
         for copy in regroup:
             copy.wait_recv()
         own.wait()
-        halos.append(low_halo(psi.at[0]))
-        halos.append(high_halo(psi.at[0]))
-
-    for step in range(STEPS):
-        solve(step, regrouped if step == 0 else lambda: None)
-        for copy in spread_potential(step):
-            copy.wait_recv()
-        spread = spread_halo(step)
-        for copy in halos:
-            copy.wait_recv()
-
+
+        def reorder(p, carry):
+            for c in range(2):
+                psi[0, c, WIDE + p] = gathered(land, c, p)
+            return carry
+
+        lax.fori_loop(0, GROUP, reorder, 0)
+
+    plans = (
+        {"near": ("begin",), "source": ("end", (0, 2)), "again": ((2, 3),), "solved": ((5, 3),)},
+        {"source": ((0, 2),), "again": ((2, 3),), "solved": ((5, 3),)},
+    )
+
+    def meanwhile(step, place):
+        for what in plans[step].get(place, ()):
+            if what == "begin":
+                begin_regroup()
+            elif what == "end":
+                regrouped()
+            else:
+                halos[what] = halo(step, *what)
+
+    def clear_outside(step, begin, count):
         @pl.when(g == 0)
         def _():
-            clear_halo(0, (psi.at[step],))
+            clear_halo(WIDE - begin - count, count, (psi.at[step],))
 
         @pl.when(g == GROUPS - 1)
         def _():
-            clear_halo(WIDE + GROUP, (psi.at[step],))
-
+            clear_halo(WIDE + GROUP + begin, count, (psi.at[step],))
+
+    for step in range(STEPS):
+        meanwhile(step, "start")
+        solve(step, functools.partial(meanwhile, step))
+        meanwhile(step, "solved")
+        spread = spread_potential(step)
+        meanwhile(step, "spread")
+        for copy in spread:
+            copy.wait_recv()
+        spread = spread_halo(step)
+        meanwhile(step, "beside")
+        ready = [halos.pop(key) for key in sorted(halos)]
+        for copy in ready[0]:
+            copy.wait_recv()
+        clear_outside(step, 0, 2)
         inside(step)
+        for copy in sum(ready[1:], []):
+            copy.wait_recv()
+        clear_outside(step, 2, 6)
         for copy in spread:
             copy.wait_recv()
         later = psi.at[step + 1]
@@ -458,12 +563,9 @@
             )
         low_edge(step)
         shares.begin(0, RING // 2)
-        if step < STEPS - 1:
-            halos = [high_halo(later)]
         high_edge(step)
         shares.begin(RING // 2, RING)
         if step < STEPS - 1:
-            halos.append(low_halo(later))
             shares.wait()
             for p in range(SLAB):
                 total = ringpart[SLAB * x + p]
@@ -471,7 +573,8 @@
                     total = total + ringpart[GROUP + SLAB * (k - 1) + p]
                 part[step + 1, p] = total
 
-    hartree_out[...] = vb[WIDE : WIDE + SLAB]
+    for p in range(SLAB):
+        scatter(hartree_out, vb[WIDE + p], p)
     final = psi.at[STEPS]
     own = pltpu.make_async_copy(
         final.at[:, pl.ds(group_at, SLAB)], psi_out.at[:, x], local_sem.at[1]
@@ -489,6 +592,7 @@
     smem = pl.BlockSpec(memory_space=pltpu.SMEM)
     fields = pltpu.VMEM((2, EXT, NY, NZ), f32)
     slab = pltpu.VMEM((STEPS, SLAB, NY, NZ), f32)
+    slab_one = pltpu.VMEM((SLAB, NY, NZ), f32)
     mid = pltpu.VMEM((SLABS + 2, Y1, NZ), f32)
     low = pltpu.VMEM((SLABS + 2, Y2, NZ), f32)
     return pl.pallas_call(
@@ -509,12 +613,12 @@
             pltpu.VMEM((STEPS, FEXT, NY, NZ), f32),
             pltpu.VMEM((FEXT, NY, NZ), f32),
             pltpu.VMEM((FEXT, NY, NZ), f32),
-            pltpu.VMEM((STEPS, 2, SLABS, Y1, NZ), f32),
+            pltpu.VMEM((STEPS, 2, SLABS, 2, Y2, NZ), f32),
             mid, mid, low, low,
             pltpu.VMEM((SLABS, Y1, NZ), f32),
             pltpu.VMEM((SLABS, Y2, NZ), f32),
-            pltpu.VMEM((NY, NZ), f32),
-            pltpu.VMEM((SLABS * Y1, NZ), f32),
+            pltpu.VMEM((2, GROUP, NY, NZ), f32),
+            slab_one,
             pltpu.VMEM((SLABS, Y2, NZ), f32),
             pltpu.VMEM((10, NY, NZ), f32),
             pltpu.SemaphoreType.DMA((COPIES,)),

time: 187 us -> 175 us (0.936)
  the two profiles are of different devices: /device:TPU:68 before, /device:TPU:94 now
where the time goes in v3:
time: 175 us; the launch traced here: 173 us
  Pallas kernels  170 us (97%)
  local copies, waits for them, and re-layouts  3 us (2%)
    pallas_call x1, Pallas kernels, per_device(): pl.pallas_call(kernel, out_shape=(jax.ShapeDtypeStruct(orbitals.shape, f3...  170 us

profile of v3, /device:TPU:94, one launch (start us, length us, event | category | flops | bytes accessed | tf_op | source)
XLA Modules:
  0.0 173.2 jit_solution(4121633686213676508)
XLA Ops:
  0.6 169.6 %shard_map.59 = (f32[2,4,4,64,128]{4,3,2,1,0:T(8,128)}, f32[4,64,128]{2,1,0:T(8,128)}) custom-call(f32[2,4,4,64,128]{4,3,2,1,0:T(8,128)} %psi_in.1, s32[4]{0:T(128)} %occ.1, f32[4,64,128]{2,1,0:T(8,128)} %ext.1, f32[2]{0:T(128)} %control.1), custom_call_target="tpu_custom_call" | custom-call | tf_op jit(solution)/shard_map/pallas_call | solution.py:598
  170.2 0.0 copy-start
  170.2 2.3 %copy.8 = f32[2,4,4,64,128]{4,3,2,1,0:T(8,128)} copy(f32[2,4,4,64,128]{4,3,2,1,0:T(8,128)} %get-tuple-element.4) | data formatting | bytes 2097152
  172.6 0.0 copy-done
  172.6 0.7 copy.9
Async XLA Ops:
  170.2 2.4 %copy-start = (f32[4,64,128]{2,1,0:T(8,128)S(1)}, f32[4,64,128]{2,1,0:T(8,128)}, u32[]{:S(2)}) copy-start(f32[4,64,128]{2,1,0:T(8,128)} %get-tuple-element.5) | copy-start | bytes 393220

commit v4 on v3

--- a/solution.py
+++ b/solution.py
@@ -244,22 +244,15 @@
         copies = []
         reach = REACH if cycle == 0 else REACH - 1
         for k in range(1, reach + 1):
-            src = c1.at[step, cycle, REACH, core]
-            low = c1.at[step, cycle, REACH - k, core]
-            high = c1.at[step, cycle, REACH + k, core]
+            src = c1.at[step, cycle, REACH]
+            low = c1.at[step, cycle, REACH - k]
+            high = c1.at[step, cycle, REACH + k]
             copies.append(push(src, low, o, lax.rem(d + k, DOM)))
             copies.append(push(src, high, o, lax.rem(d + DOM - k, DOM)))
         return copies
 
     def whole_source(step, cycle, copies):
         for copy in copies:
-            copy.wait_recv()
-        reach = len(copies) // 2
-        swaps = []
-        for begin in (REACH - reach, REACH + 1):
-            piece = c1.at[step, cycle, pl.ds(begin, reach), core]
-            swaps.append(push(piece, piece, sibling, d))
-        for copy in swaps:
             copy.wait_recv()
 
     def coarse_solve(step, cycle, lo, hi):
@@ -376,15 +369,24 @@
             place = (SLAB * d + p).astype(jnp.float32)
             dipole = (place + 0.5) * (2.0 / NX) - 1.0
             pot[step, group_at + p] = gathered(ext, p) + vb[WIDE + p] + control[step] * dipole
-        src = pot.at[step, pl.ds(group_at, SLAB)]
+        src = pot.at[step, pl.ds(group_at + 2 * core, 2)]
         return [push(src, src, o, RING * g + mate(k)) for k in range(1, RING)]
+
+    def swap_potential(step):
+        pieces = [pot.at[step, pl.ds(WIDE + SLAB * mate(k) + 2 * core, 2)] for k in range(1, RING)]
+        return [push(piece, piece, sibling, d) for piece in pieces]
 
     def spread_halo(step):
         at = pot.at[step]
         return [
-            push(at.at[pl.ds(WIDE + GROUP - 6, 6)], at.at[pl.ds(WIDE - 6, 6)], o, after_group),
-            push(at.at[pl.ds(WIDE, 6)], at.at[pl.ds(WIDE + GROUP, 6)], o, before_group),
+            push(at.at[pl.ds(WIDE + GROUP - 6 + 3 * core, 3)], at.at[pl.ds(WIDE - 6 + 3 * core, 3)], o, after_group),
+            push(at.at[pl.ds(WIDE + 3 * core, 3)], at.at[pl.ds(WIDE + GROUP + 3 * core, 3)], o, before_group),
         ]
+
+    def swap_halo(step):
+        at = pot.at[step]
+        pieces = [at.at[pl.ds(WIDE - 6 + 3 * core, 3)], at.at[pl.ds(WIDE + GROUP + 3 * core, 3)]]
+        return [push(piece, piece, sibling, d) for piece in pieces]
 
     def halo(step, begin, count):
         ref = psi.at[step]
@@ -508,8 +510,8 @@
         lax.fori_loop(0, GROUP, reorder, 0)
 
     plans = (
-        {"near": ("begin",), "source": ("end", (0, 2)), "again": ((2, 3),), "solved": ((5, 3),)},
-        {"source": ((0, 2),), "again": ((2, 3),), "solved": ((5, 3),)},
+        {'near': ('begin',), 'source': ('end', (0, 2)), 'again': ((2, 2),), 'solved': ((4, 4),)},
+        {'source': ((0, 2),), 'again': ((2, 2),), 'solved': ((4, 4),)},
     )
 
     def meanwhile(step, place):
@@ -538,6 +540,8 @@
         meanwhile(step, "spread")
         for copy in spread:
             copy.wait_recv()
+        for copy in swap_potential(step):
+            copy.wait_recv()
         spread = spread_halo(step)
         meanwhile(step, "beside")
         ready = [halos.pop(key) for key in sorted(halos)]
@@ -549,6 +553,8 @@
             copy.wait_recv()
         clear_outside(step, 2, 6)
         for copy in spread:
+            copy.wait_recv()
+        for copy in swap_halo(step):
             copy.wait_recv()
         later = psi.at[step + 1]
         if step < STEPS - 1:

time: 175 us -> 170 us (0.971)
  the two profiles are of different devices: /device:TPU:94 before, /device:TPU:7 now
where the time goes in v4:
time: 170 us
  Pallas kernels  166 us (98%)
  local copies, waits for them, and re-layouts  3 us (2%)
    pallas_call x1, Pallas kernels, per_device(): pl.pallas_call(kernel, out_shape=(jax.ShapeDtypeStruct(orbitals.shape, f3...  166 us

profile of v4, /device:TPU:7, one launch (start us, length us, event | category | flops | bytes accessed | tf_op | source)
XLA Modules:
  0.0 169.6 jit_solution(17653849633861768125)
XLA Ops:
  0.6 166.0 %shard_map.59 = (f32[2,4,4,64,128]{4,3,2,1,0:T(8,128)}, f32[4,64,128]{2,1,0:T(8,128)}) custom-call(f32[2,4,4,64,128]{4,3,2,1,0:T(8,128)} %psi_in.1, s32[4]{0:T(128)} %occ.1, f32[4,64,128]{2,1,0:T(8,128)} %ext.1, f32[2]{0:T(128)} %control.1), custom_call_target="tpu_custom_call" | custom-call | tf_op jit(solution)/shard_map/pallas_call | solution.py:604
  166.6 0.0 copy-start
  166.6 2.3 %copy.8 = f32[2,4,4,64,128]{4,3,2,1,0:T(8,128)} copy(f32[2,4,4,64,128]{4,3,2,1,0:T(8,128)} %get-tuple-element.4) | data formatting | bytes 2097152
  169.0 0.0 copy-done
  169.0 0.7 copy.9
Async XLA Ops:
  166.6 2.4 %copy-start = (f32[4,64,128]{2,1,0:T(8,128)S(1)}, f32[4,64,128]{2,1,0:T(8,128)}, u32[]{:S(2)}) copy-start(f32[4,64,128]{2,1,0:T(8,128)} %get-tuple-element.5) | copy-start | bytes 393220

commit v5 on v4

--- a/solution.py
+++ b/solution.py
@@ -510,8 +510,8 @@
         lax.fori_loop(0, GROUP, reorder, 0)
 
     plans = (
-        {'near': ('begin',), 'source': ('end', (0, 2)), 'again': ((2, 2),), 'solved': ((4, 4),)},
-        {'source': ((0, 2),), 'again': ((2, 2),), 'solved': ((4, 4),)},
+        {"near": ("begin",), "source": ("end", (0, 2)), "again": ((2, 3),), "solved": ((5, 3),)},
+        {"source": ((0, 2),), "again": ((2, 3),), "solved": ((5, 3),)},
     )
 
     def meanwhile(step, place):

time: 170 us -> 168 us (0.988)
  the two profiles are of different devices: /device:TPU:7 before, /device:TPU:94 now
where the time goes in v5:
time: 168 us
  Pallas kernels  165 us (98%)
  local copies, waits for them, and re-layouts  3 us (2%)
    pallas_call x1, Pallas kernels, per_device(): pl.pallas_call(kernel, out_shape=(jax.ShapeDtypeStruct(orbitals.shape, f3...  165 us

profile of v5, /device:TPU:94, one launch (start us, length us, event | category | flops | bytes accessed | tf_op | source)
XLA Modules:
  0.0 168.2 jit_solution(17615404770597829141)
XLA Ops:
  0.6 164.5 %shard_map.59 = (f32[2,4,4,64,128]{4,3,2,1,0:T(8,128)}, f32[4,64,128]{2,1,0:T(8,128)}) custom-call(f32[2,4,4,64,128]{4,3,2,1,0:T(8,128)} %psi_in.1, s32[4]{0:T(128)} %occ.1, f32[4,64,128]{2,1,0:T(8,128)} %ext.1, f32[2]{0:T(128)} %control.1), custom_call_target="tpu_custom_call" | custom-call | tf_op jit(solution)/shard_map/pallas_call | solution.py:604
  165.2 0.0 copy-start
  165.2 2.3 %copy.8 = f32[2,4,4,64,128]{4,3,2,1,0:T(8,128)} copy(f32[2,4,4,64,128]{4,3,2,1,0:T(8,128)} %get-tuple-element.4) | data formatting | bytes 2097152
  167.5 0.0 copy-done
  167.5 0.7 copy.9
Async XLA Ops:
  165.2 2.4 %copy-start = (f32[4,64,128]{2,1,0:T(8,128)S(1)}, f32[4,64,128]{2,1,0:T(8,128)}, u32[]{:S(2)}) copy-start(f32[4,64,128]{2,1,0:T(8,128)} %get-tuple-element.5) | copy-start | bytes 393220
